TPU v7x, 32 devices: a whole 2x2x4 slice. The times are simulated.
32 devices in a mesh: grp: 4 (over y, core), tile: 8 (over z, x).
Axes of the slice: x: 2, y: 2, z: 4, core: 2. Of those that a mesh axis runs over, the one named last changes fastest.
Arguments:
- amplitudes: bfloat16 [256, 4, 9216], P(('grp', 'tile')), may hold values from -6 to 6
- kept: int32 [256, 4], P(('grp', 'tile')), may hold values from 0 to 7, all different within a row; in each aligned block of 8 rows (0 to 7, 8 to 15, ...) at most 8 rows name the same one
- coef: bfloat16 [256], P(('grp', 'tile')), may hold values from -0.125 to 0.125
- ladder_factor: bfloat16 [8, 16, 96, 96], P('tile'), may hold values from -0.375 to 0.375
- cycle_integral_tiles: bfloat16 [8, 96, 96], P('tile'), may hold values from -0.625 to 0.625
Outputs:
- residual: bfloat16 [256, 4, 9216], P(('grp', 'tile'))
Inputs may be any that keep to these rules, and one draw needn't show every extreme that they name: `kept`: each row names 4 different tiles; in each aligned block of 8 rows (the pairs of one device) no tile is named by more than 8 rows, a bound that some block reaches.
All inputs are finite; a program needn't handle non-finite values.
Results may differ from a plain program's by a relative error of at most 0.0056.
Values may be sent and summed in bfloat16 or wider, within the bound.
No kernel may reach another device: no remote copies, remote signals or barrier semaphores. Data moves between devices by JAX's collectives and lax.ppermute only.
A program may use at most 128 MiB of HBM per device.

v0:
```python
import jax
import jax.numpy as jnp
from jax import lax
from jax.sharding import PartitionSpec as P


def build_blocks(block_list, factors, hidden_state):
    total = jnp.einsum(
        "vsab,vbc->vsac", block_list, hidden_state, preferred_element_type=jnp.float32
    )
    for number in range(factors.shape[1]):
        factor = factors[:, number]
        inner = jnp.einsum(
            "vsab,vcb->vsac", block_list, factor, preferred_element_type=jnp.float32
        ).astype(jnp.bfloat16)
        total = total + jnp.einsum(
            "vda,vsac->vsdc", factor, inner, preferred_element_type=jnp.float32
        )
    return total.astype(jnp.bfloat16)


def on_device(amplitudes, kept, coef, ladder_factor, cycle_integral_tiles):
    pair_count, kept_count, flat_width = amplitudes.shape
    tile_width = ladder_factor.shape[-1]
    tile_count = lax.axis_size("tile")
    capacity = 2 * pair_count * kept_count // tile_count
    flat_tiles = kept.reshape(-1)
    matches = (flat_tiles[:, None] == jnp.arange(tile_count, dtype=jnp.int32)[None, :]).astype(
        jnp.int32
    )
    earlier = jnp.cumsum(matches, axis=0) - matches
    slots = jnp.sum(earlier * matches, axis=1)
    block_list = amplitudes.reshape(pair_count * kept_count, flat_width)
    scales = jnp.repeat(coef, kept_count)
    buffer = (
        jnp.zeros((tile_count, capacity, flat_width), jnp.bfloat16)
        .at[flat_tiles, slots]
        .set(block_list)
    )
    weights = jnp.zeros((tile_count, capacity), jnp.bfloat16).at[flat_tiles, slots].set(scales)
    arrived, arrived_weights = (
        lax.all_to_all(buffer, "tile", split_axis=0, concat_axis=0, tiled=True),
        lax.all_to_all(weights, "tile", split_axis=0, concat_axis=0, tiled=True),
    )
    partial_sum = jnp.einsum(
        "vs,vsx->x", arrived_weights, arrived, preferred_element_type=jnp.float32
    )
    cycle_total = lax.psum(partial_sum, "grp")
    cycle_running_sum = cycle_total.reshape(1, tile_width, tile_width).astype(jnp.bfloat16)
    hidden_state = jnp.einsum(
        "rwq,rqj->rwj", cycle_running_sum, cycle_integral_tiles, preferred_element_type=jnp.float32
    ).astype(jnp.bfloat16)
    local = arrived.reshape(1, tile_count * capacity, tile_width, tile_width)
    result = build_blocks(local, ladder_factor, hidden_state)
    returned = lax.all_to_all(
        result.reshape(tile_count, capacity, flat_width),
        "tile",
        split_axis=0,
        concat_axis=0,
        tiled=True,
    )
    residual = returned[flat_tiles, slots]
    return residual.reshape(pair_count, kept_count, flat_width)


def solution(mesh):
    in_specs = (
        P(("grp", "tile"), None, None),
        P(("grp", "tile"), None),
        P(("grp", "tile")),
        P("tile", None, None, None),
        P("tile", None, None),
    )
    out_specs = P(("grp", "tile"), None, None)
    return jax.shard_map(
        on_device, mesh=mesh, in_specs=in_specs, out_specs=out_specs, check_vma=False
    )
```

profile of v0, /device:TPU:0, one launch (start us, length us, event | category | flops | bytes accessed | tf_op | source)
XLA Modules:
  0.0 178.4 jit_solution(15336036399009400126)
XLA Ops:
  0.0 0.0 copy-start
  0.0 0.8 copy.77
  0.8 0.1 eq.15
  0.8 0.1 reshape.287
  0.9 0.1 fusion.84
  1.0 0.1 reduce_window_sum.11
  1.1 0.2 select_reduce_fusion
  1.2 1.2 reshape.318
  2.5 1.1 broadcast_in_dim.6
  3.6 18.4 %scatter_fusion = bf16[8,8,9216]{2,1,0:T(8,128)(2,1)} fusion(bf16[8,8,9216]{2,1,0:T(8,128)(2,1)} %broadcast_in_dim.6, s32[32]{0:T(128)S(1)} %get-tuple-element.5, bf16[32,9216]{1,0:T(8,128)(2,1)S(1)} %reshape.318), kind=kCustom, calls=%fused_computation.1 | custom fusion | bytes 1769728 | tf_op jit(solution)/shard_map/scatter | solution.py:38
  22.0 0.0 copy-start.2
  22.0 7.3 %all-to-all-start = ((bf16[8,8,9216]{2,1,0:T(8,128)(2,1)}), bf16[8,8,9216]{2,1,0:T(8,128)(2,1)S(1)}, u32[]{:S(2)}, u32[]{:S(2)}) async-start(bf16[8,8,9216]{2,1,0:T(8,128)(2,1)} %scatter_fusion), calls=%async_computation | async-start | bytes 2359296 | tf_op jit(solution)/shard_map/all_to_all | solution.py:42
  29.3 0.0 copy-done.2
  29.3 0.1 broadcast_in_dim.8
  29.4 0.1 reshape.324
  29.5 2.0 %scatter_fusion.1 = bf16[8,8]{1,0:T(8,128)(2,1)S(1)} fusion(bf16[8,8]{1,0:T(8,128)(2,1)S(1)} %broadcast_in_dim.7, s32[32]{0:T(128)S(1)} %get-tuple-element.5, bf16[32]{0:T(256)(128)(2,1)S(1)} %reshape.324), kind=kCustom, calls=%fused_computation.2 | custom fusion | bytes 448 | tf_op jit(solution)/shard_map/scatter | solution.py:40
  31.5 0.0 copy-start.1
  31.5 0.6 copy.79
  32.1 25.6 %all-to-all-done = bf16[8,8,9216]{2,1,0:T(8,128)(2,1)S(1)} async-done(((bf16[8,8,9216]{2,1,0:T(8,128)(2,1)}), bf16[8,8,9216]{2,1,0:T(8,128)(2,1)S(1)}, u32[]{:S(2)}, u32[]{:S(2)}) %all-to-all-start) | async-done | bytes 1179680 | tf_op jit(solution)/shard_map/all_to_all | solution.py:42
  57.8 3.6 %all-to-all-start.1 = ((bf16[8,1,8]{2,1,0:T(2,128)(2,1)}), bf16[8,1,8]{2,1,0:T(2,128)(2,1)S(1)}, u32[]{:S(2)}, u32[]{:S(2)}) async-start(bf16[8,1,8]{2,1,0:T(2,128)(2,1)} %copy.79), calls=%async_computation.1 | async-start | bytes 8192 | tf_op jit(solution)/shard_map/all_to_all | solution.py:43
  61.4 1.7 reshape.289
  63.1 0.0 copy-done.1
  63.1 2.8 %fusion.15 = f32[64,96,96]{1,2,0:T(8,128)} fusion(bf16[64,96,96]{2,1,0:T(8,128)(2,1)S(1)} %reshape.289, bf16[1,16,96,96]{3,2,1,0:T(8,128)(2,1)S(1)} %copy-done.1), kind=kOutput, calls=%fused_computation.50 | convolution fusion | flops 227082240 | bytes 3981312 | tf_op jit(solution)/shard_map/vda,vsac->vsdc/dot_general | solution.py:16
  65.9 2.8 %fusion.14 = f32[64,96,96]{1,2,0:T(8,128)} fusion(bf16[64,96,96]{2,1,0:T(8,128)(2,1)S(1)} %reshape.289, bf16[1,16,96,96]{3,2,1,0:T(8,128)(2,1)S(1)} %copy-done.1), kind=kOutput, calls=%fused_computation.49 | convolution fusion | flops 227082240 | bytes 3981312 | tf_op jit(solution)/shard_map/vda,vsac->vsdc/dot_general | solution.py:16
  68.7 2.8 %fusion.13 = f32[64,96,96]{1,2,0:T(8,128)} fusion(bf16[64,96,96]{2,1,0:T(8,128)(2,1)S(1)} %reshape.289, bf16[1,16,96,96]{3,2,1,0:T(8,128)(2,1)S(1)} %copy-done.1), kind=kOutput, calls=%fused_computation.48 | convolution fusion | flops 227082240 | bytes 3981312 | tf_op jit(solution)/shard_map/vda,vsac->vsdc/dot_general | solution.py:16
  71.5 2.7 %fusion.12 = f32[64,96,96]{1,2,0:T(8,128)} fusion(bf16[64,96,96]{2,1,0:T(8,128)(2,1)S(1)} %reshape.289, bf16[1,16,96,96]{3,2,1,0:T(8,128)(2,1)S(1)} %copy-done.1), kind=kOutput, calls=%fused_computation.47 | convolution fusion | flops 227082240 | bytes 3981312 | tf_op jit(solution)/shard_map/vda,vsac->vsdc/dot_general | solution.py:16
  74.2 2.8 %fusion.11 = f32[64,96,96]{1,2,0:T(8,128)} fusion(bf16[64,96,96]{2,1,0:T(8,128)(2,1)S(1)} %reshape.289, bf16[1,16,96,96]{3,2,1,0:T(8,128)(2,1)S(1)} %copy-done.1), kind=kOutput, calls=%fused_computation.46 | convolution fusion | flops 227082240 | bytes 3981312 | tf_op jit(solution)/shard_map/vda,vsac->vsdc/dot_general | solution.py:16
  77.0 2.8 %fusion.10 = f32[64,96,96]{1,2,0:T(8,128)} fusion(bf16[64,96,96]{2,1,0:T(8,128)(2,1)S(1)} %reshape.289, bf16[1,16,96,96]{3,2,1,0:T(8,128)(2,1)S(1)} %copy-done.1), kind=kOutput, calls=%fused_computation.45 | convolution fusion | flops 227082240 | bytes 3981312 | tf_op jit(solution)/shard_map/vda,vsac->vsdc/dot_general | solution.py:16
  79.7 2.8 %fusion.9 = f32[64,96,96]{1,2,0:T(8,128)} fusion(bf16[64,96,96]{2,1,0:T(8,128)(2,1)S(1)} %reshape.289, bf16[1,16,96,96]{3,2,1,0:T(8,128)(2,1)S(1)} %copy-done.1), kind=kOutput, calls=%fused_computation.44 | convolution fusion | flops 227082240 | bytes 3981312 | tf_op jit(solution)/shard_map/vda,vsac->vsdc/dot_general | solution.py:16
  82.5 2.8 %fusion.8 = f32[64,96,96]{1,2,0:T(8,128)} fusion(bf16[64,96,96]{2,1,0:T(8,128)(2,1)S(1)} %reshape.289, bf16[1,16,96,96]{3,2,1,0:T(8,128)(2,1)S(1)} %copy-done.1), kind=kOutput, calls=%fused_computation.43 | convolution fusion | flops 227082240 | bytes 3981312 | tf_op jit(solution)/shard_map/vda,vsac->vsdc/dot_general | solution.py:16
  85.3 2.9 %fusion.7 = f32[64,96,96]{1,2,0:T(8,128)} fusion(bf16[64,96,96]{2,1,0:T(8,128)(2,1)S(1)} %reshape.289, bf16[1,16,96,96]{3,2,1,0:T(8,128)(2,1)S(1)} %copy-done.1), kind=kOutput, calls=%fused_computation.42 | convolution fusion | flops 227082240 | bytes 3981312 | tf_op jit(solution)/shard_map/vda,vsac->vsdc/dot_general | solution.py:16
  88.1 2.9 %fusion.6 = f32[64,96,96]{1,2,0:T(8,128)} fusion(bf16[64,96,96]{2,1,0:T(8,128)(2,1)S(1)} %reshape.289, bf16[1,16,96,96]{3,2,1,0:T(8,128)(2,1)S(1)} %copy-done.1), kind=kOutput, calls=%fused_computation.41 | convolution fusion | flops 227082240 | bytes 3981312 | tf_op jit(solution)/shard_map/vda,vsac->vsdc/dot_general | solution.py:16
  91.0 2.7 %fusion.5 = f32[64,96,96]{1,2,0:T(8,128)} fusion(bf16[64,96,96]{2,1,0:T(8,128)(2,1)S(1)} %reshape.289, bf16[1,16,96,96]{3,2,1,0:T(8,128)(2,1)S(1)} %copy-done.1), kind=kOutput, calls=%fused_computation.40 | convolution fusion | flops 227082240 | bytes 3981312 | tf_op jit(solution)/shard_map/vda,vsac->vsdc/dot_general | solution.py:16
  93.7 3.0 %fusion.4 = f32[64,96,96]{1,2,0:T(8,128)} fusion(bf16[64,96,96]{2,1,0:T(8,128)(2,1)S(1)} %reshape.289, bf16[1,16,96,96]{3,2,1,0:T(8,128)(2,1)S(1)} %copy-done.1), kind=kOutput, calls=%fused_computation.39 | convolution fusion | flops 227082240 | bytes 3981312 | tf_op jit(solution)/shard_map/vda,vsac->vsdc/dot_general | solution.py:16
  96.7 2.7 %fusion.3 = f32[64,96,96]{1,2,0:T(8,128)} fusion(bf16[64,96,96]{2,1,0:T(8,128)(2,1)S(1)} %reshape.289, bf16[1,16,96,96]{3,2,1,0:T(8,128)(2,1)S(1)} %copy-done.1), kind=kOutput, calls=%fused_computation.38 | convolution fusion | flops 227082240 | bytes 3981312 | tf_op jit(solution)/shard_map/vda,vsac->vsdc/dot_general | solution.py:16
  99.5 2.8 %fusion.2 = f32[64,96,96]{1,2,0:T(8,128)} fusion(bf16[64,96,96]{2,1,0:T(8,128)(2,1)S(1)} %reshape.289, bf16[1,16,96,96]{3,2,1,0:T(8,128)(2,1)S(1)} %copy-done.1), kind=kOutput, calls=%fused_computation.37 | convolution fusion | flops 227082240 | bytes 3981312 | tf_op jit(solution)/shard_map/vda,vsac->vsdc/dot_general | solution.py:16
  102.3 2.8 %fusion.1 = f32[64,96,96]{1,2,0:T(8,128)} fusion(bf16[64,96,96]{2,1,0:T(8,128)(2,1)S(1)} %reshape.289, bf16[1,16,96,96]{3,2,1,0:T(8,128)(2,1)S(1)} %copy-done.1), kind=kOutput, calls=%fused_computation.36 | convolution fusion | flops 227082240 | bytes 3981312 | tf_op jit(solution)/shard_map/vda,vsac->vsdc/dot_general | solution.py:16
  105.1 0.0 all-to-all-done.1
  105.1 0.5 fusion.85
  105.5 11.8 %psum.7 = bf16[9216]{0:T(1024)(128)(2,1)S(1)} all-reduce(f32[9216]{0:T(1024)S(1)} %bitcast.242), channel_id=1, replica_groups=mesh['grp'=4,'tile'=8] {'grp'}, use_global_device_ids=true, to_apply=%region_4.5 | all-reduce | flops 9216 | bytes 55296 | tf_op jit(solution)/shard_map/psum | solution.py:48
  117.4 0.1 convert_element_type.85
  117.5 0.0 copy-done
  117.5 2.3 %fusion.17 = f32[64,96,96]{2,1,0:T(8,128)} fusion(bf16[64,96,96]{2,1,0:T(8,128)(2,1)S(1)} %reshape.289, bf16[96,96]{1,0:T(8,128)(2,1)S(1)} %convert_element_type.85, bf16[1,96,96]{2,1,0:T(8,128)(2,1)S(1)} %copy-done), kind=kOutput, calls=%fused_computation.53 | convolution fusion | flops 115024896 | bytes 3575808 | tf_op jit(solution)/shard_map/vsab,vbc->vsac/dot_general | solution.py:8
  119.8 18.4 %fusion = bf16[1,64,96,96]{3,2,1,0:T(8,128)(2,1)S(1)} fusion(f32[64,96,96]{1,2,0:T(8,128)} %fusion.15, f32[64,96,96]{1,2,0:T(8,128)} %fusion.14, f32[64,96,96]{1,2,0:T(8,128)} %fusion.13, f32[64,96,96]{1,2,0:T(8,128)} %fusion.12, f32[64,96,96]{1,2,0:T(8,128)} %fusion.11, f32[64,96,96]{1,2,0:T(8,128)} %fusion.10, f32[64,96,96]{1,2,0:T(8,128)} %fusion.9, ...), kind=kOutput, calls=%fused_computation.4 | convolution fusion | flops 237109248 | bytes 52740096 | tf_op jit(solution)/shard_map/vda,vsac->vsdc/dot_general | solution.py:16
  138.2 3.0 %reshape.308 = bf16[8,8,9216]{2,1,0:T(8,128)(2,1)} reshape(bf16[1,64,96,96]{3,2,1,0:T(8,128)(2,1)S(1)} %fusion) | data formatting | bytes 2359296 | tf_op jit(solution)/shard_map/reshape | solution.py:56
  141.2 33.8 %all_to_all.22 = bf16[8,8,9216]{2,1,0:T(8,128)(2,1)S(1)} all-to-all(bf16[8,8,9216]{2,1,0:T(8,128)(2,1)} %reshape.308), channel_id=1, replica_groups=mesh['grp'=4,'tile'=8] {'tile'}, dimensions={0} | all-to-all | bytes 2359296 | tf_op jit(solution)/shard_map/all_to_all | solution.py:55
  175.0 2.3 %gather_fusion = bf16[32,9216]{1,0:T(8,128)(2,1)S(1)} fusion(bf16[8,8,9216]{2,1,0:T(8,128)(2,1)S(1)} %all_to_all.22, s32[32]{0:T(128)S(1)} %bitcast.241), kind=kCustom, calls=%fused_computation | custom fusion | bytes 1179904 | tf_op jit(solution)/shard_map/gather | solution.py:62
  177.3 1.0 reshape.309
  (2 shorter events, 0.0 us)
Async XLA Ops:
  0.0 117.5 %copy-start = (bf16[1,96,96]{2,1,0:T(8,128)(2,1)S(1)}, bf16[1,96,96]{2,1,0:T(8,128)(2,1)}, u32[]{:S(2)}) copy-start(bf16[1,96,96]{2,1,0:T(8,128)(2,1)} %param.9) | copy-start | bytes 55300
  22.0 7.3 %copy-start.2 = (bf16[8]{0:T(256)(128)(2,1)S(1)}, bf16[8]{0:T(256)(128)(2,1)}, u32[]{:S(2)}) copy-start(bf16[8]{0:T(256)(128)(2,1)} %param.7) | copy-start | bytes 52
  22.0 35.8 %all-to-all-start = ((bf16[8,8,9216]{2,1,0:T(8,128)(2,1)}), bf16[8,8,9216]{2,1,0:T(8,128)(2,1)S(1)}, u32[]{:S(2)}, u32[]{:S(2)}) async-start(bf16[8,8,9216]{2,1,0:T(8,128)(2,1)} %scatter_fusion), calls=%async_computation | async-start | bytes 2359296 | tf_op jit(solution)/shard_map/all_to_all | solution.py:42
  31.5 31.6 %copy-start.1 = (bf16[1,16,96,96]{3,2,1,0:T(8,128)(2,1)S(1)}, bf16[1,16,96,96]{3,2,1,0:T(8,128)(2,1)}, u32[]{:S(2)}) copy-start(bf16[1,16,96,96]{3,2,1,0:T(8,128)(2,1)} %param.8) | copy-start | bytes 884740
  57.8 47.3 %all-to-all-start.1 = ((bf16[8,1,8]{2,1,0:T(2,128)(2,1)}), bf16[8,1,8]{2,1,0:T(2,128)(2,1)S(1)}, u32[]{:S(2)}, u32[]{:S(2)}) async-start(bf16[8,1,8]{2,1,0:T(2,128)(2,1)} %copy.79), calls=%async_computation.1 | async-start | bytes 8192 | tf_op jit(solution)/shard_map/all_to_all | solution.py:43
where the time goes:
time: 179 us; the launch traced here: 178 us
  matrix products  63.1 us (35%)
  blocking collectives  45.7 us (26%)
  local copies, waits for them, and re-layouts  32.6 us (18%)
  waiting for transfers between devices  25.6 us (14%)
  starting transfers between devices  10.9 us (6%)
    dot_general x16, matrix products, build_blocks(): jnp.einsum('vda,vsac->vsdc', factor, inner, preferred_element_type=jnp.fl...  60.3 us
    all_to_all x1, blocking collectives, on_device(): lax.all_to_all(result.reshape(tile_count, capacity, flat_width), 'tile',...  33.8 us
    all_to_all x1, waiting for transfers between devices, on_device(): lax.all_to_all(buffer, 'tile', split_axis=0, concat_axis=0, tiled=True)  25.6 us
    scatter x1, local copies, waits for them, and re-layouts, on_device(): buffer = jnp.zeros((tile_count, capacity, flat_width), jnp.bfloat16).at[f...  18.4 us
    psum x1, blocking collectives, on_device(): cycle_total = lax.psum(partial_sum, 'grp')  11.8 us
    all_to_all x1, starting transfers between devices, on_device(): lax.all_to_all(buffer, 'tile', split_axis=0, concat_axis=0, tiled=True)  7.32 us
    all_to_all x1, starting transfers between devices, on_device(): lax.all_to_all(weights, 'tile', split_axis=0, concat_axis=0, tiled=True)  3.59 us
  transfers between devices with their start and end apart: 2, of which 1 were waited for; matrix products, arithmetic and copies ran while one was open for 26% of the time, Pallas kernels for 0%

commit v1 on v0

v1 whole, which is shorter than its diff:
```python
import functools

import jax
import jax.numpy as jnp
from jax import lax
from jax.experimental import pallas as pl
from jax.experimental.pallas import tpu as pltpu
from jax.sharding import PartitionSpec as P

LANES = 128
ALL = ("grp", "tile")


def pack_factors(factors):
    count, width, _ = factors.shape
    quads = factors.reshape(count // 4, 4, width, width)
    spare = LANES - width
    pieces = [quads[:, 3, :, i * spare:(i + 1) * spare] for i in range(3)]
    packed = jnp.concatenate([quads[:, :3], jnp.stack(pieces, axis=1)], axis=-1)
    return packed.reshape(2, count // 8 * 3, width, LANES)


def unpack(refs, stacked, beside, width):
    spare = LANES - width
    lane = lax.broadcasted_iota(jnp.int32, (width, LANES), 1)
    number = 0
    for ref in refs:
        for quad in range(ref.shape[0] // 3):
            parts = [ref[quad * 3 + i] for i in range(3)]
            wide = [part.astype(jnp.float32) for part in parts]
            moved = [pltpu.roll(wide[i], spare * (i + 1), 1) for i in range(3)]
            fourth = jnp.where(lane < spare, moved[0], jnp.where(lane < 2 * spare, moved[1], moved[2]))
            parts.append(fourth.astype(jnp.bfloat16))
            for part in parts:
                stacked[number * width:(number + 1) * width, :] = part
                beside[:, number * LANES:(number + 1) * LANES] = part
                number += 1


def ladder_kernel(tiles, width, kept_ref, me_ref, blocks_ref, hidden_ref, *rest):
    factor_refs, out_ref = rest[:2 * tiles], rest[2 * tiles]
    table, counts, stacked, beside, grown = rest[2 * tiles + 1:]
    rows = blocks_ref.shape[0]
    most = table.shape[0] // tiles
    me = me_ref[0]

    def clear(j, _):
        counts[j] = 0
        return 0

    lax.fori_loop(0, tiles, clear, 0)

    def fill(r, _):
        slot = kept_ref[r] ^ me
        n = counts[slot]
        table[slot * most + n] = r
        counts[slot] = n + 1
        return 0

    lax.fori_loop(0, rows, fill, 0)

    factor_count = stacked.shape[0] // width
    for slot in range(tiles):
        count = counts[slot]

        @pl.when(count > 0)
        def _(slot=slot, count=count):
            unpack(factor_refs[2 * slot:2 * slot + 2], stacked, beside, width)
            hidden = hidden_ref[slot ^ me]

            def job(i, _):
                first = table[slot * most + 2 * i]
                second = table[slot * most + jnp.minimum(2 * i + 1, count - 1)]
                left, right = blocks_ref[first], blocks_ref[second]
                pair = jnp.concatenate([left, right], axis=1)
                inner = jnp.dot(stacked[...], pair, preferred_element_type=jnp.float32)
                for f in range(factor_count):
                    part = inner[f * width:(f + 1) * width].astype(jnp.bfloat16)
                    grown[0:width, f * LANES:(f + 1) * LANES] = part[:, :LANES]
                    grown[width:2 * width, f * LANES:(f + 1) * LANES] = part[:, LANES:]
                total = lax.dot_general(
                    grown[...], beside[...], (((1,), (1,)), ((), ())), preferred_element_type=jnp.float32
                )
                both = jnp.concatenate([left[:width], right[:width]], axis=0)
                total = total + jnp.dot(both, hidden, preferred_element_type=jnp.float32)
                total = total.astype(jnp.bfloat16)
                out_ref[first] = total[:width]
                out_ref[second] = total[width:]
                return 0

            lax.fori_loop(0, (count + 1) // 2, job, 0)


def ladder(kept, me, blocks, hidden, parts, tiles, width, most):
    rows = blocks.shape[0]
    factor_count = parts[0].shape[0] // 3 * 4 * 2
    smem, vmem = pl.BlockSpec(memory_space=pltpu.SMEM), pl.BlockSpec(memory_space=pltpu.VMEM)
    return pl.pallas_call(
        functools.partial(ladder_kernel, tiles, width),
        out_shape=jax.ShapeDtypeStruct((rows, width, width), jnp.bfloat16),
        in_specs=[smem, smem] + [vmem] * (2 + len(parts)),
        out_specs=vmem,
        scratch_shapes=[
            pltpu.SMEM((tiles * most,), jnp.int32),
            pltpu.SMEM((tiles,), jnp.int32),
            pltpu.VMEM((factor_count * width, LANES), jnp.bfloat16),
            pltpu.VMEM((width, factor_count * LANES), jnp.bfloat16),
            pltpu.VMEM((2 * width, factor_count * LANES), jnp.bfloat16),
        ],
        compiler_params=pltpu.CompilerParams(vmem_limit_bytes=48 << 20),
        cost_estimate=pl.CostEstimate(flops=rows * factor_count * 4 * width**3, bytes_accessed=4 << 20, transcendentals=0),
    )(kept, me, blocks, hidden, *parts)


def on_device(amplitudes, kept, coef, ladder_factor, cycle_integral_tiles):
    pairs, slots, flat = amplitudes.shape
    width = ladder_factor.shape[-1]
    tiles, groups = lax.axis_size("tile"), lax.axis_size("grp")
    across = 1 << ((tiles.bit_length() - 1) // 2)
    rows = pairs * slots
    me = lax.axis_index("tile")
    core = lax.axis_index("grp") % 2

    def to_tile(array, flip):
        return lax.ppermute(array, "tile", [(i, i ^ flip) for i in range(tiles)])

    def to_core(array):
        return lax.ppermute(array, "grp", [(i, i ^ 1) for i in range(groups)])

    packed = pack_factors(ladder_factor[0])
    mine = lax.dynamic_index_in_dim(packed, core, 0, keepdims=False)
    halves = {0: mine}
    for up in range(1, tiles // across):
        halves[up * across] = to_tile(mine, up * across)
    for up in range(tiles // across):
        for side in range(1, across):
            halves[up * across + side] = to_tile(halves[up * across], side)
    parts = []
    for slot in range(tiles):
        if slot == 0:
            parts += [packed[0], packed[1]]
        else:
            parts += [halves[slot], to_core(halves[slot])]

    block_list = amplitudes.reshape(rows, flat)
    names = kept.reshape(rows)
    weights = jnp.where(
        jnp.arange(tiles, dtype=jnp.int32)[:, None] == names[None, :], jnp.repeat(coef, slots)[None, :], jnp.zeros((), coef.dtype)
    )
    part_sum = jnp.dot(weights, block_list, preferred_element_type=jnp.float32)
    share = flat // groups
    shares = part_sum.reshape(tiles, groups, share).transpose(1, 0, 2).reshape(groups * tiles, share)
    arrived = lax.all_to_all(shares, ALL, split_axis=0, concat_axis=0, tiled=True)
    running = jnp.sum(arrived, axis=0).astype(jnp.bfloat16).reshape(width // groups, width)
    hidden = jnp.dot(running, cycle_integral_tiles[0], preferred_element_type=jnp.float32).astype(jnp.bfloat16)
    hidden = jnp.pad(hidden, ((0, 0), (0, LANES - width)))
    spread = lax.all_to_all(
        jnp.broadcast_to(hidden[None], (groups * tiles,) + hidden.shape), ALL, split_axis=0, concat_axis=0, tiled=True
    )
    hidden = spread.reshape(groups, tiles, width // groups, LANES).transpose(1, 0, 2, 3).reshape(tiles, width, LANES)
    hidden = jnp.pad(hidden, ((0, 0), (0, LANES - width), (0, 0)))[:, :, :width]

    blocks = jnp.pad(block_list.reshape(rows, width, width), ((0, 0), (0, LANES - width), (0, LANES - width)))
    residual = ladder(names, me.reshape(1), blocks, hidden, parts, tiles, width, pairs)
    return residual.reshape(pairs, slots, flat)


def solution(mesh):
    in_specs = (
        P(("grp", "tile"), None, None),
        P(("grp", "tile"), None),
        P(("grp", "tile")),
        P("tile", None, None, None),
        P("tile", None, None),
    )
    out_specs = P(("grp", "tile"), None, None)
    return jax.shard_map(
        on_device, mesh=mesh, in_specs=in_specs, out_specs=out_specs, check_vma=False
    )
```

time: 179 us -> 76.6 us (0.43)
  matrix products: 63.1 us -> 0.32 us
  blocking collectives: 45.7 us -> 0 us
  Pallas kernels: 0 us -> 16.7 us
  local copies, waits for them, and re-layouts: 32.6 us -> 20 us
  starting transfers between devices: 10.9 us -> 21.9 us
  waiting for transfers between devices: 25.6 us -> 17.1 us
    dot_general x18 -> x2, matrix products: 63.1 us -> 0.32 us  [the longest x1 0.19 us: on_device(): part_sum = jnp.dot(weights, block_list, preferred_element_type=jnp.float32)]
    all_to_all x1 -> x0, blocking collectives: 33.8 us -> none  [on_device(): lax.all_to_all(result.reshape(tile_count, capacity, flat_width), 'tile',...]
    all_to_all x2, waiting for transfers between devices: 25.6 us -> 2.23 us  [the longest x1 2.23 us: on_device(): lax.all_to_all(jnp.broadcast_to(hidden[None], (groups * tiles,) + hidden....]
    scatter x2 -> x0, local copies, waits for them, and re-layouts: 20.5 us -> none  [the longest x1 18.4 us: on_device(): buffer = jnp.zeros((tile_count, capacity, flat_width), jnp.bfloat16).at[f...]
    pallas_call x0 -> x1, Pallas kernels: none -> 16.7 us  [ladder(): pl.pallas_call(functools.partial(ladder_kernel, tiles, width), out_shape=...]
    ppermute x0 -> x14, waiting for transfers between devices: none -> 14.9 us  [the longest x7 14.9 us: to_tile(): return lax.ppermute(array, 'tile', [(i, i ^ flip) for i in range(tiles)])]
    psum x1 -> x0, blocking collectives: 11.8 us -> none  [on_device(): cycle_total = lax.psum(partial_sum, 'grp')]
    ppermute x0 -> x14, starting transfers between devices: none -> 10.9 us  [the longest x7 9.79 us: to_tile(): return lax.ppermute(array, 'tile', [(i, i ^ flip) for i in range(tiles)])]
  transfers between devices with their start and end apart: 2 -> 16, of which waited for: 1 -> 4; matrix products, arithmetic and copies ran while one was open for 26% -> 9% of each run, Pallas kernels for 0% -> 0%
where the time goes in v1:
time: 76.6 us
  starting transfers between devices  21.9 us (29%)
  local copies, waits for them, and re-layouts  20 us (26%)
  waiting for transfers between devices  17.1 us (22%)
  Pallas kernels  16.7 us (22%)
    pallas_call x1, Pallas kernels, ladder(): pl.pallas_call(functools.partial(ladder_kernel, tiles, width), out_shape=...  16.7 us
    ppermute x7, waiting for transfers between devices, to_tile(): return lax.ppermute(array, 'tile', [(i, i ^ flip) for i in range(tiles)])  14.9 us
    ppermute x7, starting transfers between devices, to_tile(): return lax.ppermute(array, 'tile', [(i, i ^ flip) for i in range(tiles)])  9.79 us
    unnamed x35, local copies, waits for them, and re-layouts  9.06 us
    all_to_all x1, starting transfers between devices, on_device(): lax.all_to_all(shares, ALL, split_axis=0, concat_axis=0, tiled=True)  7.3 us
    all_to_all x1, starting transfers between devices, on_device(): lax.all_to_all(jnp.broadcast_to(hidden[None], (groups * tiles,) + hidden....  3.73 us
    all_to_all x1, waiting for transfers between devices, on_device(): lax.all_to_all(jnp.broadcast_to(hidden[None], (groups * tiles,) + hidden....  2.23 us
    reshape x1, local copies, waits for them, and re-layouts, on_device(): return residual.reshape(pairs, slots, flat)  1.94 us
  transfers between devices with their start and end apart: 16, of which 4 were waited for; matrix products, arithmetic and copies ran while one was open for 9% of the time, Pallas kernels for 0%

profile of v1, /device:TPU:0, one launch (start us, length us, event | category | flops | bytes accessed | tf_op | source)
XLA Modules:
  0.0 76.6 jit_solution(13073380714364367618)
XLA Ops:
  0.0 0.7 broadcast_in_dim.24
  0.8 0.1 broadcast_in_dim.25
  0.8 0.1 copy.10
  1.0 1.2 %reshape.45 = bf16[32,9216]{1,0:T(8,128)(2,1)S(1)} reshape(bf16[8,4,9216]{2,1,0:T(4,128)(2,1)} %param.5) | data formatting | bytes 1179648 | tf_op jit(solution)/shard_map/reshape | solution.py:145
  2.2 0.2 convolution_bitcast_fusion
  2.4 1.0 %copy.12 = f32[32,1,2304]{2,1,0:T(1,128)} copy(f32[32,1,2304]{2,0,1:T(8,128)S(1)} %convolution_bitcast_fusion) | data formatting | bytes 589824 | tf_op jit(solution)/shard_map/all_to_all | solution.py:153
  3.4 7.3 %all-to-all-start = ((f32[32,1,2304]{2,1,0:T(1,128)}), f32[32,1,2304]{2,1,0:T(1,128)S(1)}, u32[]{:S(2)}, u32[]{:S(2)}) async-start(f32[32,1,2304]{2,1,0:T(1,128)} %copy.12), calls=%async_computation | async-start | bytes 589824 | tf_op jit(solution)/shard_map/all_to_all | solution.py:153
  10.8 0.2 copy.14
  11.0 0.1 maximum_maximum_fusion
  11.2 0.2 copy.18
  11.3 3.7 %collective-permute-start.10 = (bf16[6,96,128]{2,1,0:T(8,128)(2,1)S(1)}, bf16[6,96,128]{2,1,0:T(8,128)(2,1)S(1)}, u32[]{:S(2)}, u32[]{:S(2)}) collective-permute-start(bf16[6,96,128]{2,1,0:T(8,128)(2,1)S(1)} %bitcast.33), channel_id=1, source_target_pairs={{0,6},{1,7},{2,4},{3,5},{4,2},{5,3},{6,0},{7,1},{8,14},{9,15},{10,... | collective-permute-start | bytes 442376 | tf_op jit(solution)/shard_map/ppermute | solution.py:125
  15.0 0.8 collective-permute-start.2
  15.8 1.8 %collective-permute-start = (bf16[6,96,128]{2,1,0:T(8,128)(2,1)S(1)}, bf16[6,96,128]{2,1,0:T(8,128)(2,1)S(1)}, u32[]{:S(2)}, u32[]{:S(2)}) collective-permute-start(bf16[6,96,128]{2,1,0:T(8,128)(2,1)S(1)} %bitcast.36), channel_id=1, source_target_pairs={{0,1},{1,0},{2,3},{3,2},{4,5},{5,4},{6,7},{7,6},{8,9},{9,8},{10,11... | collective-permute-start | bytes 442376 | tf_op jit(solution)/shard_map/ppermute | solution.py:125
  17.5 6.3 %collective-permute-done.10.rest_12_ = bf16[6,96,128]{2,1,0:T(8,128)(2,1)S(1)} collective-permute-done((bf16[6,96,128]{2,1,0:T(8,128)(2,1)S(1)}, bf16[6,96,128]{2,1,0:T(8,128)(2,1)S(1)}, u32[]{:S(2)}, u32[]{:S(2)}) %collective-permute-start.10) | collective-permute-done | bytes 147488 | tf_op jit(solution)/shard_map/ppermute | solution.py:125
  23.8 1.5 %collective-permute-start.12 = (bf16[6,96,128]{2,1,0:T(8,128)(2,1)S(1)}, bf16[6,96,128]{2,1,0:T(8,128)(2,1)S(1)}, u32[]{:S(2)}, u32[]{:S(2)}) collective-permute-start(bf16[6,96,128]{2,1,0:T(8,128)(2,1)S(1)} %collective-permute-done.10.rest_12_), channel_id=1, source_target_pairs={{0,1},{1,0},{2,3},{3,2},{4,5},{5,4},{6,7},{7,6},{8,9},{9,8},{10,11... | collective-permute-start | bytes 442376 | tf_op jit(solution)/shard_map/ppermute | solution.py:125
  25.3 8.2 %collective-permute-done.6.rest_8_ = bf16[6,96,128]{2,1,0:T(8,128)(2,1)S(1)} collective-permute-done((bf16[6,96,128]{2,1,0:T(8,128)(2,1)S(1)}, bf16[6,96,128]{2,1,0:T(8,128)(2,1)S(1)}, u32[]{:S(2)}, u32[]{:S(2)}) %collective-permute-start.6) | collective-permute-done | bytes 147488 | tf_op jit(solution)/shard_map/ppermute | solution.py:125
  33.5 1.5 %collective-permute-start.8 = (bf16[6,96,128]{2,1,0:T(8,128)(2,1)S(1)}, bf16[6,96,128]{2,1,0:T(8,128)(2,1)S(1)}, u32[]{:S(2)}, u32[]{:S(2)}) collective-permute-start(bf16[6,96,128]{2,1,0:T(8,128)(2,1)S(1)} %collective-permute-done.6.rest_8_), channel_id=1, source_target_pairs={{0,1},{1,0},{2,3},{3,2},{4,5},{5,4},{6,7},{7,6},{8,9},{9,8},{10,11... | collective-permute-start | bytes 442376 | tf_op jit(solution)/shard_map/ppermute | solution.py:125
  34.9 0.2 reduce_sum.9
  35.1 0.1 convert_element_type.23
  35.3 0.6 collective-permute-start.4
  35.9 0.1 convolution_convert_fusion
  36.0 0.7 broadcast_in_dim.28
  36.8 3.7 %all-to-all-start.1 = ((bf16[32,24,128]{2,1,0:T(8,128)(2,1)}), bf16[32,24,128]{2,1,0:T(8,128)(2,1)}, u32[]{:S(2)}, u32[]{:S(2)}) async-start(bf16[32,24,128]{2,1,0:T(8,128)(2,1)} %broadcast_in_dim.28), calls=%async_computation.1 | async-start | bytes 393216 | tf_op jit(solution)/shard_map/all_to_all | solution.py:157
  40.5 0.3 collective-permute-start.3
  40.8 0.3 collective-permute-start.1
  41.1 0.2 collective-permute-start.13
  41.3 0.3 collective-permute-start.9
  41.6 0.4 collective-permute-done.4.rest_6_
  42.0 0.8 fusion.10
  42.8 1.5 %reshape_reshape.3 = bf16[32,96,96]{2,1,0:T(8,128)(2,1)} reshape(bf16[8,4,9216]{2,1,0:T(4,128)(2,1)S(1)} %copy-done.11) | data formatting | bytes 1179648 | tf_op jit(solution)/shard_map/reshape;reshape | solution.py:163
  44.3 0.2 copy.16
  44.5 0.8 copy-done.12
  45.2 0.2 copy.15
  45.4 1.4 %pad.12.blocks_ref = bf16[32,128,128]{2,1,0:T(8,128)(2,1)S(1)} pad(bf16[32,96,96]{2,1,0:T(8,128)(2,1)} %reshape_reshape.3, bf16[]{:T(256)} %constant.25.clone.1), padding=0_0x0_32x0_32 | pad | bytes 1638402 | tf_op jit(solution)/shard_map/jit(_pad)/pad | solution.py:163
  46.8 2.2 %all-to-all-done.1 = bf16[32,24,128]{2,1,0:T(8,128)(2,1)} async-done(((bf16[32,24,128]{2,1,0:T(8,128)(2,1)}), bf16[32,24,128]{2,1,0:T(8,128)(2,1)}, u32[]{:S(2)}, u32[]{:S(2)}) %all-to-all-start.1) | async-done | bytes 196640 | tf_op jit(solution)/shard_map/all_to_all | solution.py:157
  49.0 0.9 %copy.13 = bf16[8,4,24,128]{3,2,1,0:T(8,128)(2,1)S(1)} copy(bf16[8,4,24,128]{3,2,0,1:T(8,128)(2,1)} %bitcast.7) | data formatting | bytes 393216 | tf_op jit(solution)/shard_map/transpose | solution.py:160
  50.0 0.6 copy-done.1
  50.7 0.7 copy-done.3
  51.4 0.7 copy-done.5
  52.0 0.7 copy-done.7
  52.7 0.6 copy-done.9
  53.3 0.9 %copy-done.2 = bf16[6,96,128]{2,1,0:T(8,128)(2,1)S(1)} copy-done((bf16[6,96,128]{2,1,0:T(8,128)(2,1)S(1)}, bf16[6,96,128]{2,1,0:T(8,128)(2,1)}, u32[]{:S(2)}) %copy-start.2) | copy-done | bytes 147480
  54.2 0.9 %copy-done.4 = bf16[6,96,128]{2,1,0:T(8,128)(2,1)S(1)} copy-done((bf16[6,96,128]{2,1,0:T(8,128)(2,1)S(1)}, bf16[6,96,128]{2,1,0:T(8,128)(2,1)}, u32[]{:S(2)}) %copy-start.4) | copy-done | bytes 147480
  55.1 0.9 %copy-done.6 = bf16[6,96,128]{2,1,0:T(8,128)(2,1)S(1)} copy-done((bf16[6,96,128]{2,1,0:T(8,128)(2,1)S(1)}, bf16[6,96,128]{2,1,0:T(8,128)(2,1)}, u32[]{:S(2)}) %copy-start.6) | copy-done | bytes 147480
  56.1 0.9 %copy-done.8 = bf16[6,96,128]{2,1,0:T(8,128)(2,1)S(1)} copy-done((bf16[6,96,128]{2,1,0:T(8,128)(2,1)S(1)}, bf16[6,96,128]{2,1,0:T(8,128)(2,1)}, u32[]{:S(2)}) %copy-start.8) | copy-done | bytes 147480
  57.0 0.9 %copy-done.10 = bf16[6,96,128]{2,1,0:T(8,128)(2,1)S(1)} copy-done((bf16[6,96,128]{2,1,0:T(8,128)(2,1)S(1)}, bf16[6,96,128]{2,1,0:T(8,128)(2,1)}, u32[]{:S(2)}) %copy-start.10) | copy-done | bytes 147480
  57.9 16.7 %shard_map.55 = bf16[32,96,96]{2,1,0:T(8,128)(2,1)S(1)} custom-call(s32[32]{0:T(128)S(1)} %reshape.43.kept_ref, s32[1]{0:T(128)} %bitcast.me_ref, bf16[32,128,128]{2,1,0:T(8,128)(2,1)S(1)} %pad.12.blocks_ref, bf16[8,128,96]{2,1,0:T(8,128)(2,1)S(1)} %pad_slice_fusion.hidden_ref, bf16[6,96,128]{2,1,0:T(8,128)(2,1)S(1)} %bitcast.27, ...), custom_call_target="tpu_custom_call" | custom-call | flops 1811939328 | bytes 4194304 | tf_op jit(solution)/shard_map/pallas_call | solution.py:98
  74.6 1.9 %reshape.49 = bf16[8,4,9216]{2,1,0:T(4,128)(2,1)} reshape(bf16[32,96,96]{2,1,0:T(8,128)(2,1)S(1)} %shard_map.55) | data formatting | bytes 1179648 | tf_op jit(solution)/shard_map/reshape | solution.py:165
  (43 shorter events, 0.3 us)
Async XLA Ops:
  0.0 35.9 %copy-start = (bf16[1,96,96]{2,1,0:T(8,128)(2,1)S(1)}, bf16[1,96,96]{2,1,0:T(8,128)(2,1)}, u32[]{:S(2)}) copy-start(bf16[1,96,96]{2,1,0:T(8,128)(2,1)} %param.9) | copy-start | bytes 55300
  0.0 0.8 %copy-start.15 = (s32[8,4]{0,1:T(4,128)S(1)}, s32[8,4]{0,1:T(4,128)}, u32[]{:S(2)}) copy-start(s32[8,4]{0,1:T(4,128)} %param.6) | copy-start | bytes 388
  3.4 7.3 %copy-start.14 = (bf16[1,16,96,96]{3,2,1,0:T(8,128)(2,1)S(1)}, bf16[1,16,96,96]{3,2,1,0:T(8,128)(2,1)}, u32[]{:S(2)}) copy-start(bf16[1,16,96,96]{3,2,1,0:T(8,128)(2,1)} %param.8) | copy-start | bytes 884740
  3.4 31.5 %all-to-all-start = ((f32[32,1,2304]{2,1,0:T(1,128)}), f32[32,1,2304]{2,1,0:T(1,128)S(1)}, u32[]{:S(2)}, u32[]{:S(2)}) async-start(f32[32,1,2304]{2,1,0:T(1,128)} %copy.12), calls=%async_computation | async-start | bytes 589824 | tf_op jit(solution)/shard_map/all_to_all | solution.py:153
  11.3 12.5 %collective-permute-start.10 = (bf16[6,96,128]{2,1,0:T(8,128)(2,1)S(1)}, bf16[6,96,128]{2,1,0:T(8,128)(2,1)S(1)}, u32[]{:S(2)}, u32[]{:S(2)}) collective-permute-start(bf16[6,96,128]{2,1,0:T(8,128)(2,1)S(1)} %bitcast.33), channel_id=1, source_target_pairs={{0,6},{1,7},{2,4},{3,5},{4,2},{5,3},{6,0},{7,1},{8,14},{9,15},{10,... | collective-permute-start | bytes 442376 | tf_op jit(solution)/shard_map/ppermute | solution.py:125
  15.0 18.5 %collective-permute-start.6 = (bf16[6,96,128]{2,1,0:T(8,128)(2,1)S(1)}, bf16[6,96,128]{2,1,0:T(8,128)(2,1)S(1)}, u32[]{:S(2)}, u32[]{:S(2)}) collective-permute-start(bf16[6,96,128]{2,1,0:T(8,128)(2,1)S(1)} %bitcast.34), channel_id=1, source_target_pairs={{0,4},{1,5},{2,6},{3,7},{4,0},{5,1},{6,2},{7,3},{8,12},{9,13},{10,... | collective-permute-start | bytes 442376 | tf_op jit(solution)/shard_map/ppermute | solution.py:125
  15.0 20.2 %collective-permute-start.2 = (bf16[6,96,128]{2,1,0:T(8,128)(2,1)S(1)}, bf16[6,96,128]{2,1,0:T(8,128)(2,1)S(1)}, u32[]{:S(2)}, u32[]{:S(2)}) collective-permute-start(bf16[6,96,128]{2,1,0:T(8,128)(2,1)S(1)} %bitcast.35), channel_id=1, source_target_pairs={{0,2},{1,3},{2,0},{3,1},{4,6},{5,7},{6,4},{7,5},{8,10},{9,11},{10,... | collective-permute-start | bytes 442376 | tf_op jit(solution)/shard_map/ppermute | solution.py:125
  15.8 19.5 %collective-permute-start = (bf16[6,96,128]{2,1,0:T(8,128)(2,1)S(1)}, bf16[6,96,128]{2,1,0:T(8,128)(2,1)S(1)}, u32[]{:S(2)}, u32[]{:S(2)}) collective-permute-start(bf16[6,96,128]{2,1,0:T(8,128)(2,1)S(1)} %bitcast.36), channel_id=1, source_target_pairs={{0,1},{1,0},{2,3},{3,2},{4,5},{5,4},{6,7},{7,6},{8,9},{9,8},{10,11... | collective-permute-start | bytes 442376 | tf_op jit(solution)/shard_map/ppermute | solution.py:125
  23.8 16.7 %collective-permute-start.12 = (bf16[6,96,128]{2,1,0:T(8,128)(2,1)S(1)}, bf16[6,96,128]{2,1,0:T(8,128)(2,1)S(1)}, u32[]{:S(2)}, u32[]{:S(2)}) collective-permute-start(bf16[6,96,128]{2,1,0:T(8,128)(2,1)S(1)} %collective-permute-done.10.rest_12_), channel_id=1, source_target_pairs={{0,1},{1,0},{2,3},{3,2},{4,5},{5,4},{6,7},{7,6},{8,9},{9,8},{10,11... | collective-permute-start | bytes 442376 | tf_op jit(solution)/shard_map/ppermute | solution.py:125
  25.3 15.5 %collective-permute-start.11 = (bf16[6,96,128]{2,1,0:T(8,128)(2,1)S(1)}, bf16[6,96,128]{2,1,0:T(8,128)(2,1)S(1)}, u32[]{:S(2)}, u32[]{:S(2)}) collective-permute-start(bf16[6,96,128]{2,1,0:T(8,128)(2,1)S(1)} %collective-permute-done.10.rest_12_), channel_id=1, source_target_pairs={{0,8},{8,0},{16,24},{24,16},{1,9},{9,1},{17,25},{25,17},{2,10},{10... | collective-permute-start | bytes 442376 | tf_op jit(solution)/shard_map/ppermute | solution.py:128
  33.5 7.6 %collective-permute-start.8 = (bf16[6,96,128]{2,1,0:T(8,128)(2,1)S(1)}, bf16[6,96,128]{2,1,0:T(8,128)(2,1)S(1)}, u32[]{:S(2)}, u32[]{:S(2)}) collective-permute-start(bf16[6,96,128]{2,1,0:T(8,128)(2,1)S(1)} %collective-permute-done.6.rest_8_), channel_id=1, source_target_pairs={{0,1},{1,0},{2,3},{3,2},{4,5},{5,4},{6,7},{7,6},{8,9},{9,8},{10,11... | collective-permute-start | bytes 442376 | tf_op jit(solution)/shard_map/ppermute | solution.py:125
  35.2 6.1 %collective-permute-start.7 = (bf16[6,96,128]{2,1,0:T(8,128)(2,1)S(1)}, bf16[6,96,128]{2,1,0:T(8,128)(2,1)S(1)}, u32[]{:S(2)}, u32[]{:S(2)}) collective-permute-start(bf16[6,96,128]{2,1,0:T(8,128)(2,1)S(1)} %collective-permute-done.6.rest_8_), channel_id=1, source_target_pairs={{0,8},{8,0},{16,24},{24,16},{1,9},{9,1},{17,25},{25,17},{2,10},{10... | collective-permute-start | bytes 442376 | tf_op jit(solution)/shard_map/ppermute | solution.py:128
  35.3 6.7 %collective-permute-start.4 = (bf16[6,96,128]{2,1,0:T(8,128)(2,1)S(1)}, bf16[6,96,128]{2,1,0:T(8,128)(2,1)S(1)}, u32[]{:S(2)}, u32[]{:S(2)}) collective-permute-start(bf16[6,96,128]{2,1,0:T(8,128)(2,1)S(1)} %collective-permute-done.2.rest_4_), channel_id=1, source_target_pairs={{0,1},{1,0},{2,3},{3,2},{4,5},{5,4},{6,7},{7,6},{8,9},{9,8},{10,11... | collective-permute-start | bytes 442376 | tf_op jit(solution)/shard_map/ppermute | solution.py:125
  36.8 6.0 %copy-start.11 = (bf16[8,4,9216]{2,1,0:T(4,128)(2,1)S(1)}, bf16[8,4,9216]{2,1,0:T(4,128)(2,1)}, u32[]{:S(2)}) copy-start(bf16[8,4,9216]{2,1,0:T(4,128)(2,1)} %param.5) | copy-start | bytes 1769476
  36.8 12.3 %all-to-all-start.1 = ((bf16[32,24,128]{2,1,0:T(8,128)(2,1)}), bf16[32,24,128]{2,1,0:T(8,128)(2,1)}, u32[]{:S(2)}, u32[]{:S(2)}) async-start(bf16[32,24,128]{2,1,0:T(8,128)(2,1)} %broadcast_in_dim.28), calls=%async_computation.1 | async-start | bytes 393216 | tf_op jit(solution)/shard_map/all_to_all | solution.py:157
  40.5 9.5 %collective-permute-start.3 = (bf16[6,96,128]{2,1,0:T(8,128)(2,1)S(1)}, bf16[6,96,128]{2,1,0:T(8,128)(2,1)S(1)}, u32[]{:S(2)}, u32[]{:S(2)}) collective-permute-start(bf16[6,96,128]{2,1,0:T(8,128)(2,1)S(1)} %collective-permute-done.2.rest_4_), channel_id=1, source_target_pairs={{0,8},{8,0},{16,24},{24,16},{1,9},{9,1},{17,25},{25,17},{2,10},{10... | collective-permute-start | bytes 442376 | tf_op jit(solution)/shard_map/ppermute | solution.py:128
  40.8 9.9 %collective-permute-start.1 = (bf16[6,96,128]{2,1,0:T(8,128)(2,1)S(1)}, bf16[6,96,128]{2,1,0:T(8,128)(2,1)S(1)}, u32[]{:S(2)}, u32[]{:S(2)}) collective-permute-start(bf16[6,96,128]{2,1,0:T(8,128)(2,1)S(1)} %collective-permute-done.rest_2_), channel_id=1, source_target_pairs={{0,8},{8,0},{16,24},{24,16},{1,9},{9,1},{17,25},{25,17},{2,10},{10... | collective-permute-start | bytes 442376 | tf_op jit(solution)/shard_map/ppermute | solution.py:128
  41.1 10.3 %collective-permute-start.13 = (bf16[6,96,128]{2,1,0:T(8,128)(2,1)S(1)}, bf16[6,96,128]{2,1,0:T(8,128)(2,1)S(1)}, u32[]{:S(2)}, u32[]{:S(2)}) collective-permute-start(bf16[6,96,128]{2,1,0:T(8,128)(2,1)S(1)} %collective-permute-done.12.rest_14_), channel_id=1, source_target_pairs={{0,8},{8,0},{16,24},{24,16},{1,9},{9,1},{17,25},{25,17},{2,10},{10... | collective-permute-start | bytes 442376 | tf_op jit(solution)/shard_map/ppermute | solution.py:128
  41.3 10.7 %collective-permute-start.9 = (bf16[6,96,128]{2,1,0:T(8,128)(2,1)S(1)}, bf16[6,96,128]{2,1,0:T(8,128)(2,1)S(1)}, u32[]{:S(2)}, u32[]{:S(2)}) collective-permute-start(bf16[6,96,128]{2,1,0:T(8,128)(2,1)S(1)} %collective-permute-done.8.rest_10_), channel_id=1, source_target_pairs={{0,8},{8,0},{16,24},{24,16},{1,9},{9,1},{17,25},{25,17},{2,10},{10... | collective-permute-start | bytes 442376 | tf_op jit(solution)/shard_map/ppermute | solution.py:128
  42.0 10.7 %collective-permute-start.5 = (bf16[6,96,128]{2,1,0:T(8,128)(2,1)S(1)}, bf16[6,96,128]{2,1,0:T(8,128)(2,1)S(1)}, u32[]{:S(2)}, u32[]{:S(2)}) collective-permute-start(bf16[6,96,128]{2,1,0:T(8,128)(2,1)S(1)} %collective-permute-done.4.rest_6_), channel_id=1, source_target_pairs={{0,8},{8,0},{16,24},{24,16},{1,9},{9,1},{17,25},{25,17},{2,10},{10... | collective-permute-start | bytes 442376 | tf_op jit(solution)/shard_map/ppermute | solution.py:128
  42.8 1.5 %copy-start.13 = (bf16[2,3,96,128]{2,3,1,0:T(8,128)(2,1)S(1)}, bf16[2,3,96,128]{2,3,1,0:T(8,128)(2,1)}, u32[]{:S(2)}) copy-start(bf16[2,3,96,128]{2,3,1,0:T(8,128)(2,1)} %get-tuple-element.5) | copy-start | bytes 442372
  44.3 0.9 %copy-start.12 = (bf16[2,3,96,128]{2,3,1,0:T(8,128)(2,1)S(1)}, bf16[2,3,96,128]{2,3,1,0:T(8,128)(2,1)}, u32[]{:S(2)}) copy-start(bf16[2,3,96,128]{2,3,1,0:T(8,128)(2,1)} %get-tuple-element.6) | copy-start | bytes 442372
  50.0 0.7 copy-start.1
  50.7 0.7 copy-start.3
  51.4 0.7 copy-start.5
  52.0 0.7 copy-start.7
  52.7 0.6 copy-start.9
  53.3 0.9 %copy-start.2 = (bf16[6,96,128]{2,1,0:T(8,128)(2,1)S(1)}, bf16[6,96,128]{2,1,0:T(8,128)(2,1)}, u32[]{:S(2)}) copy-start(bf16[6,96,128]{2,1,0:T(8,128)(2,1)} %copy-done.1) | copy-start | bytes 442372
  54.2 0.9 %copy-start.4 = (bf16[6,96,128]{2,1,0:T(8,128)(2,1)S(1)}, bf16[6,96,128]{2,1,0:T(8,128)(2,1)}, u32[]{:S(2)}) copy-start(bf16[6,96,128]{2,1,0:T(8,128)(2,1)} %copy-done.3) | copy-start | bytes 442372
  55.1 0.9 %copy-start.6 = (bf16[6,96,128]{2,1,0:T(8,128)(2,1)S(1)}, bf16[6,96,128]{2,1,0:T(8,128)(2,1)}, u32[]{:S(2)}) copy-start(bf16[6,96,128]{2,1,0:T(8,128)(2,1)} %copy-done.5) | copy-start | bytes 442372
  56.1 0.9 %copy-start.8 = (bf16[6,96,128]{2,1,0:T(8,128)(2,1)S(1)}, bf16[6,96,128]{2,1,0:T(8,128)(2,1)}, u32[]{:S(2)}) copy-start(bf16[6,96,128]{2,1,0:T(8,128)(2,1)} %copy-done.7) | copy-start | bytes 442372
  57.0 0.9 %copy-start.10 = (bf16[6,96,128]{2,1,0:T(8,128)(2,1)S(1)}, bf16[6,96,128]{2,1,0:T(8,128)(2,1)}, u32[]{:S(2)}) copy-start(bf16[6,96,128]{2,1,0:T(8,128)(2,1)} %copy-done.9) | copy-start | bytes 442372
